TPU v7x, 256 devices: a whole 4x4x8 slice. The times are simulated.
256 devices in a mesh: ctx: 32 (over x, y, core), grp: 8 (over z).
Axes of the slice: x: 4, y: 4, z: 8, core: 2. Of those that a mesh axis runs over, the one named last changes fastest.
Arguments:
- window_states: bfloat16 [8, 64, 8192], P('grp'), may hold values from -6 to 6
- query_weight: bfloat16 [8192, 8192], P('grp', 'ctx'), may hold values from -0.0625 to 0.0625
- cache_keys: bfloat16 [8, 16384, 1024], P('grp', 'ctx'), may hold values from -65 to 65
- cache_values: bfloat16 [8, 16384, 1024], P('grp', 'ctx'), may hold values from -6 to 6
- kept_blocks: int32 [8, 8, 32], P('grp', None, 'ctx'), may hold values from 0 to 127, as said below
- retained_block_count: int32 [8, 8, 32], P('grp', None, 'ctx'), may hold values from 0 to 1, as said below
- decode_queries: bfloat16 [8, 4, 32, 8192], P('grp', None, 'ctx'), may hold values from -9 to 9
- tail_keys: bfloat16 [8, 32, 64, 1024], P('grp', 'ctx'), may hold values from -6 to 6
- tail_values: bfloat16 [8, 32, 64, 1024], P('grp', 'ctx'), may hold values from -6 to 6
- row_lengths: int32 [8, 32], P('grp', 'ctx'), may hold values from 2 to 61, as said below
Outputs:
- pooled_votes: float32 [8, 8, 16384], P('grp', None, 'ctx')
- decode_out: bfloat16 [8, 4, 32, 8192], P('grp', None, 'ctx')
Inputs may be any that keep to these rules, and one draw needn't show every extreme that they name: `kept_blocks`: for key head k, entry c names one block held by ctx index c, that is one of the blocks c * 4 to c * 4 + 3; it is kept only if retained_block_count[g, k, c] is 1. `retained_block_count`: in every request some device holds 1 kept blocks for every key head. `row_lengths`: 61 is reached in every request.
All inputs are finite; a program needn't handle non-finite values.
Results may differ from a plain program's by a relative error of at most 0.0019.
Values may be sent and summed in bfloat16 or wider, within the bound.
A program may use at most 128 MiB of HBM per device.

v0:
```python
import math
import jax
import jax.numpy as jnp
from jax import lax
from jax.sharding import PartitionSpec as P

KEY_HEADS = 8
HEAD_DIMENSION = 128
BLOCK_POSITIONS = 128
POOL = 7


def combined_all(part, axis, combine):
    gathered = jax.tree.map(lambda a: lax.all_gather(a, axis), part)

    def take(source):
        return jax.tree.map(lambda a: lax.dynamic_index_in_dim(a, source, 0, False), gathered)

    return lax.fori_loop(
        1, lax.axis_size(axis), lambda source, state: combine(state, take(source)), take(0)
    )


def padded_2(cells, sides, width):
    for axis, dim in sides:
        count = lax.axis_size(axis)
        ends = count - 1
        head = lax.slice_in_dim(cells, 0, width, axis=dim)
        tail = lax.slice_in_dim(cells, cells.shape[dim] - width, cells.shape[dim], axis=dim)
        cells = jnp.concatenate(
            [
                lax.ppermute(tail, axis, [(i, (i + 1) % count) for i in range(ends)]),
                cells,
                lax.ppermute(head, axis, [((i + 1) % count, i) for i in range(ends)]),
            ],
            axis=dim,
        )
    return cells


def rotary_table(positions, head_size):
    exponent = jnp.arange(0, head_size, 2).astype(jnp.float32) / head_size
    inverse = jnp.power(jnp.float32(500000.0), -exponent)
    wavelength = 2.0 * math.pi / inverse
    smooth = (8192.0 / wavelength - 1.0) / 3.0
    blended = (1.0 - smooth) * inverse / 8.0 + smooth * inverse
    adjusted = jnp.where(
        wavelength > 8192.0, inverse / 8.0, jnp.where(wavelength < 2048.0, inverse, blended)
    )
    angles = positions[:, None] * adjusted[None, :]
    return (jnp.cos(angles), jnp.sin(angles))


def rotate(vectors, cosine_table, sine_table):
    half_size = vectors.shape[-1] // 2
    leading = vectors[..., :half_size]
    trailing = vectors[..., half_size:]
    cosine_part = cosine_table[:, None, :]
    sine_part = sine_table[:, None, :]
    return jnp.concatenate(
        [
            leading * cosine_part - trailing * sine_part,
            trailing * cosine_part + leading * sine_part,
        ],
        axis=-1,
    )


def merge_stats(earlier, later):
    highest = jnp.maximum(earlier[0], later[0])
    return (
        highest,
        earlier[1] * jnp.exp(earlier[0] - highest) + later[1] * jnp.exp(later[0] - highest),
    )


def on_device(
    window_states,
    query_weight,
    cache_keys,
    cache_values,
    kept_blocks,
    retained_block_count,
    decode_queries,
    tail_keys,
    tail_values,
    row_lengths,
):
    ctx_count = lax.axis_size("ctx")
    ctx_index = lax.axis_index("ctx")
    states = window_states[0]
    win_rows = states.shape[0]
    local_cols = query_weight.shape[1]
    local_heads = local_cols // HEAD_DIMENSION
    projected = jnp.dot(
        states,
        lax.all_gather(query_weight, "grp", axis=0, tiled=True),
        preferred_element_type=jnp.float32,
    )
    local_keys = cache_keys[0]
    ctx_local = local_keys.shape[0]
    total_ctx = ctx_local * ctx_count
    start_pos = total_ctx - win_rows
    positions = (jnp.arange(win_rows) + start_pos).astype(jnp.float32)
    cosine_table, sine_table = rotary_table(positions, HEAD_DIMENSION)
    turned = rotate(
        projected.reshape(win_rows, local_heads, HEAD_DIMENSION), cosine_table, sine_table
    )
    window_local = turned.reshape(win_rows, local_cols).astype(jnp.bfloat16)
    window_all, decode_all = (
        lax.all_gather(window_local, "ctx", axis=1, tiled=True),
        lax.all_gather(decode_queries[0], "ctx", axis=1, tiled=True),
    )
    head_total = window_all.shape[1] // HEAD_DIMENSION
    group_size = head_total // KEY_HEADS
    key_scale = 1.0 / math.sqrt(HEAD_DIMENSION)
    key_positions = ctx_index * ctx_local + jnp.arange(ctx_local)
    allowed = key_positions[None, :] <= (start_pos + jnp.arange(win_rows))[:, None]
    exp_list = []
    max_list = []
    sum_list = []
    for head_index in range(KEY_HEADS):
        head_queries = window_all[
            :,
            head_index
            * group_size
            * HEAD_DIMENSION : (head_index + 1)
            * group_size
            * HEAD_DIMENSION,
        ].reshape(win_rows, group_size, HEAD_DIMENSION)
        key_head_rows = local_keys[
            :, head_index * HEAD_DIMENSION : (head_index + 1) * HEAD_DIMENSION
        ]
        scores = (
            jnp.einsum(
                "wgd,td->gwt", head_queries, key_head_rows, preferred_element_type=jnp.float32
            )
            * key_scale
        )
        scores = jnp.where(allowed[None], scores, -1e30)
        head_max = jnp.max(scores, axis=-1)
        exponent_values = jnp.where(allowed[None], jnp.exp(scores - head_max[..., None]), 0.0)
        exp_list.append(exponent_values)
        max_list.append(head_max)
        sum_list.append(jnp.sum(exponent_values, axis=-1))
    exponentials = jnp.stack(exp_list)
    local_max = jnp.stack(max_list).reshape(head_total, win_rows)
    local_sum = jnp.stack(sum_list).reshape(head_total, win_rows)
    merged_max, merged_sum = combined_all((local_max, local_sum), "ctx", merge_stats)
    coefficient = (jnp.exp(local_max - merged_max) / merged_sum).reshape(
        KEY_HEADS, group_size, win_rows
    )
    vote_sums = jnp.sum(coefficient[..., None] * exponentials, axis=(1, 2)) * (
        total_ctx / (win_rows * group_size)
    )
    half_width = (POOL - 1) // 2
    padded = padded_2(vote_sums, (("ctx", 1),), half_width)
    pooled = padded[:, 0:ctx_local]
    for shift_index in range(1, POOL):
        pooled = pooled + padded[:, shift_index : shift_index + ctx_local]
    pooled_votes = (pooled / POOL)[None]
    step_count = decode_all.shape[0]
    rows_all = decode_all.shape[1]
    rows_local = decode_queries.shape[2]
    total_rows = step_count * rows_all
    block_total = ctx_local // BLOCK_POSITIONS
    keys_local = local_keys.reshape(block_total, BLOCK_POSITIONS, KEY_HEADS, HEAD_DIMENSION)
    values_local = cache_values[0].reshape(block_total, BLOCK_POSITIONS, KEY_HEADS, HEAD_DIMENSION)
    local_blocks = kept_blocks[0] - ctx_index * block_total
    local_counts = retained_block_count[0, :, 0]
    rounds = jnp.max(local_counts)
    grouped = decode_all.reshape(total_rows, KEY_HEADS, group_size, HEAD_DIMENSION)
    head_range = jnp.arange(KEY_HEADS)

    def visit_slot(position, state_now):
        run_max, run_sum, run_acc = state_now
        chosen = lax.dynamic_index_in_dim(local_blocks, position, 1, keepdims=False)
        key_block = keys_local[chosen, :, head_range, :]
        value_block = values_local[chosen, :, head_range, :]
        is_live = (position < local_counts)[None, :, None, None]
        scores = (
            jnp.einsum("rhgd,htd->rhgt", grouped, key_block, preferred_element_type=jnp.float32)
            * key_scale
        )
        scores = jnp.where(is_live, scores, -1e30)
        new_max = jnp.maximum(run_max, jnp.max(scores, axis=-1))
        rescale = jnp.exp(run_max - new_max)
        weights = jnp.where(is_live, jnp.exp(scores - new_max[..., None]), 0.0)
        run_sum = run_sum * rescale + jnp.sum(weights, axis=-1)
        run_acc = run_acc * rescale[..., None] + jnp.einsum(
            "rhgt,htd->rhgd",
            weights,
            value_block.astype(jnp.float32),
            precision=lax.Precision.HIGHEST,
        )
        return (new_max, run_sum, run_acc)

    initial = (
        jnp.full((total_rows, KEY_HEADS, group_size), -1e30, jnp.float32),
        jnp.zeros((total_rows, KEY_HEADS, group_size), jnp.float32),
        jnp.zeros((total_rows, KEY_HEADS, group_size, HEAD_DIMENSION), jnp.float32),
    )
    run_max, run_sum, run_acc = lax.fori_loop(0, rounds, visit_slot, initial)
    cache_max = run_max.reshape(step_count, rows_all, head_total)
    cache_sum = run_sum.reshape(step_count, rows_all, head_total)
    cache_acc = run_acc.reshape(step_count, rows_all, head_total * HEAD_DIMENSION)
    tail_len = tail_keys.shape[2]
    own_queries = decode_queries[0].reshape(
        step_count, rows_local, KEY_HEADS, group_size, HEAD_DIMENSION
    )
    tail_key_rows = tail_keys[0].reshape(rows_local, tail_len, KEY_HEADS, HEAD_DIMENSION)
    tail_value_rows = tail_values[0].reshape(rows_local, tail_len, KEY_HEADS, HEAD_DIMENSION)
    visible = (
        jnp.arange(tail_len)[None, None, :]
        < row_lengths[0][None, :, None] + jnp.arange(step_count)[:, None, None]
    )
    visible = visible[:, :, None, None, :]
    tail_scores = (
        jnp.einsum(
            "srhgd,rjhd->srhgj", own_queries, tail_key_rows, preferred_element_type=jnp.float32
        )
        * key_scale
    )
    tail_scores = jnp.where(visible, tail_scores, -1e30)
    tail_max = jnp.max(tail_scores, axis=-1)
    tail_weights = jnp.where(visible, jnp.exp(tail_scores - tail_max[..., None]), 0.0)
    tail_sum = jnp.sum(tail_weights, axis=-1).reshape(step_count, rows_local, head_total)
    tail_acc = jnp.einsum(
        "srhgj,rjhd->srhgd",
        tail_weights,
        tail_value_rows.astype(jnp.float32),
        precision=lax.Precision.HIGHEST,
    )
    tail_acc = tail_acc.reshape(step_count, rows_local, head_total, HEAD_DIMENSION)
    tail_max = tail_max.reshape(step_count, rows_local, head_total)
    received_acc, received_max, received_sum = (
        lax.all_to_all(cache_acc[None], "ctx", split_axis=2, concat_axis=0, tiled=True),
        lax.all_to_all(cache_max[None], "ctx", split_axis=2, concat_axis=0, tiled=True),
        lax.all_to_all(cache_sum[None], "ctx", split_axis=2, concat_axis=0, tiled=True),
    )
    peak_value = jnp.maximum(jnp.max(received_max, axis=0), tail_max)
    factors = jnp.exp(received_max - peak_value[None])
    tail_factor = jnp.exp(tail_max - peak_value)
    spread_acc = received_acc.reshape(
        received_acc.shape[0], step_count, rows_local, head_total, HEAD_DIMENSION
    )
    numerator = jnp.sum(spread_acc * factors[..., None], axis=0) + tail_acc * tail_factor[..., None]
    denominator = jnp.sum(received_sum * factors, axis=0) + tail_sum * tail_factor
    decode_out = (
        (numerator / denominator[..., None])
        .reshape(step_count, rows_local, head_total * HEAD_DIMENSION)
        .astype(jnp.bfloat16)[None]
    )
    return (pooled_votes, decode_out)


def solution(mesh):
    placed = (
        P("grp", None, None),
        P("grp", "ctx"),
        P("grp", "ctx", None),
        P("grp", "ctx", None),
        P("grp", None, "ctx"),
        P("grp", None, "ctx"),
        P("grp", None, "ctx", None),
        P("grp", "ctx", None, None),
        P("grp", "ctx", None, None),
        P("grp", "ctx"),
    )
    return jax.shard_map(
        on_device,
        mesh=mesh,
        in_specs=placed,
        out_specs=(P("grp", None, "ctx"), P("grp", None, "ctx", None)),
        check_vma=False,
    )
```

profile of v0, /device:TPU:25, one launch (start us, length us, event | category | flops | bytes accessed | tf_op | source)
XLA Modules:
  0.0 339.1 jit_solution(13341545864074250296)
XLA Ops:
  13.5 48.5 %all-gather.9.cloned.1.call-done = bf16[1,4,32,8192]{3,1,0,2:T(4,128)(2,1)} async-done(((bf16[1,4,1,8192]{3,1,0,2:T(4,128)(2,1)}), bf16[1,4,32,8192]{3,1,0,2:T(4,128)(2,1)}) %all-gather.9.cloned.1.call-update) | async-done | bytes 2097168 | tf_op jit(solution)/shard_map/all_gather | solution.py:112
  62.1 2.7 copy.200
  69.3 12.0 %while.34 = (s32[]{:T(128)}, f32[128,8,8]{0,2,1:T(8,128)S(1)}, f32[128,8,8]{0,2,1:T(8,128)S(1)}, f32[128,8,8,128]{3,0,2,1:T(8,128)}, s32[]{:T(128)}, /*index=5*/...) while((s32[]{:T(128)}, f32[128,8,8]{0,2,1:T(8,128)S(1)}, ...), condition=%wide.region_23.24_spmd, body=%wide.region_20.23_spmd.sunk | while | flops 1893744640 | bytes 57671904 | solution.py:203
  73.2 5.4 %bitcast_add_fusion.2 = f32[128,8,8,128]{3,0,2,1:T(8,128)S(1)} fusion(f32[128,8,8,128]{3,0,2,1:T(8,128)S(1)} %copy-done.1, f32[128,8,8]{0,2,1:T(8,128)S(1)} %get-tuple-element.508, f32[8,128,128,8]{2,1,3,0:T(8,128)S(1)} %get-tuple-element.506, f32[128,8,8]{0,2,1:T(8,128)S(1)} %max.37, pred[8]{0:T(512)(128)(4,1)S(1)} %broadcast_compare_fusion.3, ...), kind=kOutput, calls=%fused_computation.7.clone.1 | convolution fusion | flops 1616904192 | bytes 12910600 | tf_op jit(solution)/shard_map/while/body/rhgt,htd->rhgd/dot_general | solution.py:190
  82.3 5.7 %all-to-all-start.1 = ((f32[32,1,256]{2,1,0:T(1,128)}), f32[32,1,256]{2,1,0:T(1,128)S(1)}, u32[]{:S(2)}, u32[]{:S(2)}) async-start(f32[32,1,256]{2,1,0:T(1,128)} %reshape.469), calls=%async_computation.1 | async-start | bytes 65536 | tf_op jit(solution)/shard_map/all_to_all | solution.py:238
  89.0 4.6 %all-to-all-done.1 = f32[32,1,256]{2,1,0:T(1,128)S(1)} async-done(((f32[32,1,256]{2,1,0:T(1,128)}), f32[32,1,256]{2,1,0:T(1,128)S(1)}, u32[]{:S(2)}, u32[]{:S(2)}) %all-to-all-start.1) | async-done | bytes 32800 | tf_op jit(solution)/shard_map/all_to_all | solution.py:238
  93.6 5.6 %all-to-all-start.2 = ((f32[32,1,256]{2,1,0:T(1,128)}), f32[32,1,256]{2,1,0:T(1,128)S(1)}, u32[]{:S(2)}, u32[]{:S(2)}) async-start(f32[32,1,256]{2,1,0:T(1,128)} %reshape.471), calls=%async_computation.2 | async-start | bytes 65536 | tf_op jit(solution)/shard_map/all_to_all | solution.py:239
  99.2 6.6 %copy.203 = f32[128,8,8,128]{3,2,1,0:T(8,128)} copy(f32[128,8,8,128]{3,0,2,1:T(8,128)} %get-tuple-element.265) | data formatting | bytes 8388608 | tf_op jit(solution)/shard_map/while | solution.py:203
  105.9 5.0 %broadcast_in_dim_reshape.10 = f32[1,4,32,8192]{3,2,1,0:T(8,128)} reshape(f32[128,8,8,128]{3,2,1,0:T(8,128)} %copy.203) | data formatting | bytes 8388608 | tf_op jit(solution)/shard_map/broadcast_in_dim;reshape | solution.py:237
  110.8 6.9 %copy.204 = f32[1,4,32,8192]{3,1,0,2:T(4,128)} copy(f32[1,4,32,8192]{3,2,1,0:T(8,128)} %broadcast_in_dim_reshape.10) | data formatting | bytes 8388608 | tf_op jit(solution)/shard_map/broadcast_in_dim;reshape | solution.py:237
  117.8 7.7 %all-to-all-start = ((f32[1,4,32,8192]{3,1,0,2:T(4,128)}), f32[1,4,32,8192]{3,1,0,2:T(4,128)}, u32[]{:S(2)}, u32[]{:S(2)}) async-start(f32[1,4,32,8192]{3,1,0,2:T(4,128)} %copy.204), calls=%async_computation | async-start | bytes 8388608 | tf_op jit(solution)/shard_map/all_to_all | solution.py:237
  132.6 5.5 %mul.308 = f32[32,1,4,1,8192]{4,2,0,3,1:T(4,128)} reshape(f32[32,4,64,128]{3,2,1,0:T(8,128)} %mul.307) | data formatting | bytes 8388608 | tf_op jit(solution)/shard_map/mul | solution.py:247
  138.2 6.4 %copy.179 = bf16[256,8192]{1,0:T(8,128)(2,1)} copy(bf16[256,8192]{0,1:T(8,128)(2,1)} %bitcast.316) | data formatting | bytes 8388608 | tf_op jit(solution)/shard_map/dot_general | solution.py:95
  144.6 3.6 %fusion.40 = f32[64,2,128]{2,0,1:T(8,128)S(1)} fusion(bf16[2,128,8192]{2,1,0:T(8,128)(2,1)} %bitcast.313, bf16[1,64,8192]{2,1,0:T(8,128)(2,1)S(1)} %copy-done), kind=kOutput, calls=%fused_computation.69 | convolution fusion | flops 268435456 | bytes 5308416 | tf_op jit(solution)/shard_map/dot_general | solution.py:95
  149.0 29.7 %all-to-all-done = f32[1,4,32,8192]{3,1,0,2:T(4,128)} async-done(((f32[1,4,32,8192]{3,1,0,2:T(4,128)}), f32[1,4,32,8192]{3,1,0,2:T(4,128)}, u32[]{:S(2)}, u32[]{:S(2)}) %all-to-all-start) | async-done | bytes 4194336 | tf_op jit(solution)/shard_map/all_to_all | solution.py:237
  178.7 5.2 %fusion.21 = f32[4,8192]{1,0:T(4,128)S(1)} fusion(f32[32,1,4,1,8192]{4,2,0,3,1:T(4,128)} %mul.308, f32[1,4,32,8192]{3,1,0,2:T(4,128)} %all-to-all-done), kind=kLoop, calls=%fused_computation.32 | loop fusion | flops 2064384 | bytes 8519680 | tf_op jit(solution)/shard_map/reduce_sum | solution.py:247
  185.0 18.0 %all-gather.7.cloned.1.call-done = bf16[64,8192]{1,0:T(8,128)(2,1)} async-done(((bf16[64,256]{1,0:T(8,128)(2,1)}), bf16[64,8192]{1,0:T(8,128)(2,1)}) %all-gather.7.cloned.1.call-update) | async-done | bytes 1048592 | tf_op jit(solution)/shard_map/all_gather | solution.py:111
  217.5 3.6 %fusion.49 = (f32[8,64]{0,1:T(8,128)S(1)}, f32[8,64]{0,1:T(8,128)}, f32[8,64]{0,1:T(8,128)}, f32[8,64]{0,1:T(8,128)}, f32[8,64]{0,1:T(8,128)}, /*index=5*/f32[8,...) fusion(f32[8,64,512]{2,0,1:T(8,128)S(1)} %get-tuple-element.407, f32[8,64]{0,1:T(8,128)S(1)} %get-tuple-element.406, ...), kind=kLoop, calls=%fused_computation.86 | loop fusion | flops 6287360 | bytes 8454144 | tf_op jit(solution)/shard_map/reduce_sum | solution.py:145
  231.4 23.1 %all_gather.18 = f32[32,64,64]{2,1,0:T(8,128)S(1)} all-gather(f32[1,64,64]{2,1,0:T(8,128)} %bitcast.365), channel_id=1, replica_groups=mesh['ctx'=32,'grp'=8] {'ctx'}, dimensions={0}, use_global_device_ids=true | all-gather | bytes 540672 | tf_op jit(solution)/shard_map/all_gather | solution.py:14
  256.1 24.3 %all_gather.17 = f32[32,64,64]{2,1,0:T(8,128)S(1)} all-gather(f32[1,64,64]{2,1,0:T(8,128)S(1)} %bitcast.350), channel_id=1, replica_groups=mesh['ctx'=32,'grp'=8] {'ctx'}, dimensions={0}, use_global_device_ids=true | all-gather | bytes 540672 | tf_op jit(solution)/shard_map/all_gather | solution.py:14
  281.3 25.9 %while.33 = (s32[]{:T(128)}, f32[64,64]{1,0:T(8,128)S(1)}, f32[64,64]{1,0:T(8,128)S(1)}, f32[32,64,64]{2,1,0:T(8,128)}, f32[32,64,64]{2,1,0:T(8,128)}, /*index=5*/s32[]{:T(128)}, s32[]{:T(128)}, s32[]{:T(128)}) while((s32[]{:T(128)}, f32[64,64]{1,0:T(8,128)S(1)}, f32[64,64]{1,0:T(8,128)S(1)}, f32[32,64,64]{2,1,0:T(8,128)}, ...), condition=%wide.region_17.18_spmd, body=%wide.region_16.17_spmd.sunk | while | flops 24581 | bytes 98435 | solution.py:19
  317.7 3.8 %multiply_reduce_fusion = f32[8,512]{1,0:T(8,128)S(1)} fusion(f32[8,8,64,512]{3,1,2,0:T(8,128)} %bitcast_dynamic-update-slice_fusion, f32[8,8,64]{1,2,0:T(8,128)S(1)} %copy.197), kind=kLoop, calls=%fused_computation.30 | loop fusion | flops 4190208 | bytes 8421376 | tf_op jit(solution)/shard_map/reduce_sum | solution.py:153
  321.6 3.1 collective-permute-start
  326.7 5.1 %collective-permute-done.1 = f32[8,3]{1,0:T(8,128)S(1)} collective-permute-done((f32[8,3]{1,0:T(8,128)S(1)}, f32[8,3]{1,0:T(8,128)S(1)}, u32[]{:S(2)}, u32[]{:S(2)}) %collective-permute-start.1) | collective-permute-done | bytes 128 | tf_op jit(solution)/shard_map/ppermute | solution.py:34
  (223 shorter events, 91.8 us)
Async XLA Ops:
  7.2 137.4 %copy-start = (bf16[1,64,8192]{2,1,0:T(8,128)(2,1)S(1)}, bf16[1,64,8192]{2,1,0:T(8,128)(2,1)}, u32[]{:S(2)}) copy-start(bf16[1,64,8192]{2,1,0:T(8,128)(2,1)} %param.14) | copy-start | bytes 3145732
  7.2 54.9 %all-gather.9.cloned.1.call-start = ((), (), s32[]{:S(2)}) async-start(), calls=%async_computation.5 | async-start | bytes 2162688 | tf_op jit(solution)/shard_map/all_gather | solution.py:112
  7.9 130.3 %all-gather.5.cloned.1.call-start = ((), (), s32[]{:S(2)}) async-start(), calls=%async_computation.3 | async-start | bytes 4718592 | tf_op jit(solution)/shard_map/all_gather | solution.py:97
  82.3 11.3 %all-to-all-start.1 = ((f32[32,1,256]{2,1,0:T(1,128)}), f32[32,1,256]{2,1,0:T(1,128)S(1)}, u32[]{:S(2)}, u32[]{:S(2)}) async-start(f32[32,1,256]{2,1,0:T(1,128)} %reshape.469), calls=%async_computation.1 | async-start | bytes 65536 | tf_op jit(solution)/shard_map/all_to_all | solution.py:238
  93.6 24.2 %all-to-all-start.2 = ((f32[32,1,256]{2,1,0:T(1,128)}), f32[32,1,256]{2,1,0:T(1,128)S(1)}, u32[]{:S(2)}, u32[]{:S(2)}) async-start(f32[32,1,256]{2,1,0:T(1,128)} %reshape.471), calls=%async_computation.2 | async-start | bytes 65536 | tf_op jit(solution)/shard_map/all_to_all | solution.py:239
  117.7 8.6 %copy-start.24 = (bf16[1,1,64,1024]{3,2,1,0:T(8,128)(2,1)S(1)}, bf16[1,1,64,1024]{3,2,1,0:T(8,128)(2,1)}, u32[]{:S(2)}) copy-start(bf16[1,1,64,1024]{3,2,1,0:T(8,128)(2,1)} %param.21) | copy-start | bytes 393220
  117.7 8.7 %copy-start.26 = (bf16[1,4,1,8192]{3,1,2,0:T(4,128)(2,1)S(1)}, bf16[1,4,1,8192]{3,1,2,0:T(4,128)(2,1)}, u32[]{:S(2)}) copy-start(bf16[1,4,1,8192]{3,1,2,0:T(4,128)(2,1)} %param.20) | copy-start | bytes 196612
  117.7 9.4 %copy-start.25 = (bf16[1,1,64,1024]{3,2,1,0:T(8,128)(2,1)S(1)}, bf16[1,1,64,1024]{3,2,1,0:T(8,128)(2,1)}, u32[]{:S(2)}) copy-start(bf16[1,1,64,1024]{3,2,1,0:T(8,128)(2,1)} %param.22) | copy-start | bytes 393220
  117.8 61.0 %all-to-all-start = ((f32[1,4,32,8192]{3,1,0,2:T(4,128)}), f32[1,4,32,8192]{3,1,0,2:T(4,128)}, u32[]{:S(2)}, u32[]{:S(2)}) async-start(f32[1,4,32,8192]{3,1,0,2:T(4,128)} %copy.204), calls=%async_computation | async-start | bytes 8388608 | tf_op jit(solution)/shard_map/all_to_all | solution.py:237
  125.4 77.6 %all-gather.7.cloned.1.call-start = ((), (), s32[]{:S(2)}) async-start(), calls=%async_computation.4 | async-start | bytes 1081344 | tf_op jit(solution)/shard_map/all_gather | solution.py:111
  209.9 7.6 %copy-start.3 = (f32[8,64,512]{2,0,1:T(8,128)}, f32[8,64,512]{2,0,1:T(8,128)S(1)}, u32[]{:S(2)}) copy-start(f32[8,64,512]{2,0,1:T(8,128)S(1)} %get-tuple-element.399) | copy-start | bytes 3145732
  211.4 9.6 %copy-start.5 = (f32[8,64,512]{2,0,1:T(8,128)}, f32[8,64,512]{2,0,1:T(8,128)S(1)}, u32[]{:S(2)}) copy-start(f32[8,64,512]{2,0,1:T(8,128)S(1)} %get-tuple-element.401) | copy-start | bytes 3145732
  211.4 44.3 %copy-start.16 = (f32[8,64]{0,1:T(8,128)}, f32[8,64]{0,1:T(8,128)S(1)}, u32[]{:S(2)}) copy-start(f32[8,64]{0,1:T(8,128)S(1)} %get-tuple-element.400) | copy-start | bytes 6148
  213.0 8.1 %copy-start.7 = (f32[8,64,512]{2,0,1:T(8,128)}, f32[8,64,512]{2,0,1:T(8,128)S(1)}, u32[]{:S(2)}) copy-start(f32[8,64,512]{2,0,1:T(8,128)S(1)} %get-tuple-element.403) | copy-start | bytes 3145732
  213.0 42.8 %copy-start.18 = (f32[8,64]{0,1:T(8,128)}, f32[8,64]{0,1:T(8,128)S(1)}, u32[]{:S(2)}) copy-start(f32[8,64]{0,1:T(8,128)S(1)} %get-tuple-element.402) | copy-start | bytes 6148
  214.6 6.5 %copy-start.9 = (f32[8,64,512]{2,0,1:T(8,128)}, f32[8,64,512]{2,0,1:T(8,128)S(1)}, u32[]{:S(2)}) copy-start(f32[8,64,512]{2,0,1:T(8,128)S(1)} %get-tuple-element.405) | copy-start | bytes 3145732
  214.6 41.3 %copy-start.20 = (f32[8,64]{0,1:T(8,128)}, f32[8,64]{0,1:T(8,128)S(1)}, u32[]{:S(2)}) copy-start(f32[8,64]{0,1:T(8,128)S(1)} %get-tuple-element.404) | copy-start | bytes 6148
  216.2 39.8 %copy-start.22 = (f32[8,64]{0,1:T(8,128)}, f32[8,64]{0,1:T(8,128)S(1)}, u32[]{:S(2)}) copy-start(f32[8,64]{0,1:T(8,128)S(1)} %get-tuple-element.406) | copy-start | bytes 6148
  308.8 5.1 %copy-start.8 = (f32[8,64,512]{2,0,1:T(8,128)S(1)}, f32[8,64,512]{2,0,1:T(8,128)}, u32[]{:S(2)}) copy-start(f32[8,64,512]{2,0,1:T(8,128)} %copy-done.7) | copy-start | bytes 3145732
  308.8 5.1 %copy-start.19 = (f32[8,64]{0,1:T(8,128)S(1)}, f32[8,64]{0,1:T(8,128)}, u32[]{:S(2)}) copy-start(f32[8,64]{0,1:T(8,128)} %copy-done.18) | copy-start | bytes 6148
  311.4 5.1 %copy-start.12 = (f32[8,64,512]{2,0,1:T(8,128)S(1)}, f32[8,64,512]{2,0,1:T(8,128)}, u32[]{:S(2)}) copy-start(f32[8,64,512]{2,0,1:T(8,128)} %copy-done.11) | copy-start | bytes 3145732
  311.4 5.1 %copy-start.23 = (f32[8,64]{0,1:T(8,128)S(1)}, f32[8,64]{0,1:T(8,128)}, u32[]{:S(2)}) copy-start(f32[8,64]{0,1:T(8,128)} %copy-done.22) | copy-start | bytes 6148
  321.6 5.1 %collective-permute-start = (f32[8,3]{1,0:T(8,128)S(1)}, f32[8,3]{1,0:T(8,128)S(1)}, u32[]{:S(2)}, u32[]{:S(2)}) collective-permute-start(f32[8,3]{1,0:T(8,128)S(1)} %get-tuple-element.388), channel_id=1, source_target_pairs={{0,8},{8,16},{16,24},{24,32},{32,40},{40,48},{48,56},{56,64},{64,7... | collective-permute-start | bytes 296 | tf_op jit(solution)/shard_map/ppermute | solution.py:32
  324.8 7.0 %collective-permute-start.1 = (f32[8,3]{1,0:T(8,128)S(1)}, f32[8,3]{1,0:T(8,128)S(1)}, u32[]{:S(2)}, u32[]{:S(2)}) collective-permute-start(f32[8,3]{1,0:T(8,128)S(1)} %get-tuple-element.389), channel_id=1, source_target_pairs={{8,0},{16,8},{24,16},{32,24},{40,32},{48,40},{56,48},{64,56},{72,6... | collective-permute-start | bytes 296 | tf_op jit(solution)/shard_map/ppermute | solution.py:34
  (13 other events, 40.9 us)
Sparse Core Ops, SparseCore 0:
  10.6 51.4 all-gather.8
  63.9 54.1 all-gather.4
  149.1 53.8 all-gather.6
where the time goes:
time: 343 us; the launch traced here: 339 us
  waiting for transfers between devices  107 us (31%)
  local copies, waits for them, and re-layouts  65.4 us (19%)
  other arithmetic  54.6 us (16%)
  blocking collectives  47.3 us (14%)
  starting transfers between devices  24.4 us (7%)
  matrix products  22.9 us (7%)
  between operations  15.1 us (4%)
    all_gather x1, waiting for transfers between devices, on_device(): lax.all_gather(decode_queries[0], 'ctx', axis=1, tiled=True)  48.5 us
    all_gather x2, blocking collectives, combined_all(): gathered = jax.tree.map(lambda a: lax.all_gather(a, axis), part)  47.3 us
    all_to_all x1, waiting for transfers between devices, on_device(): lax.all_to_all(cache_acc[None], 'ctx', split_axis=2, concat_axis=0, tiled...  29.7 us
    add x31, other arithmetic, merge_stats(): earlier[1] * jnp.exp(earlier[0] - highest)  25.3 us
    all_gather x1, waiting for transfers between devices, on_device(): lax.all_gather(window_local, 'ctx', axis=1, tiled=True)  18 us
    unnamed x87, local copies, waits for them, and re-layouts  13.2 us
    another operation x2, local copies, waits for them, and re-layouts, on_device(): cache_acc[None]  11.9 us
    dot_general x8, matrix products, on_device(): jnp.einsum('wgd,td->gwt', head_queries, key_head_rows, preferred_element_...  11.5 us
  transfers between devices with their start and end apart: 8, of which 5 were waited for; matrix products, arithmetic and copies ran while one was open for 21% of the time, Pallas kernels for 0%

commit v1 on v0

--- a/solution.py
+++ b/solution.py
@@ -108,7 +108,9 @@
     )
     window_local = turned.reshape(win_rows, local_cols).astype(jnp.bfloat16)
     window_all, decode_all = (
-        lax.all_gather(window_local, "ctx", axis=1, tiled=True),
+        jnp.concatenate(
+            lax.all_to_all(jnp.stack([window_local] * lax.axis_size("ctx")), "ctx", 0, 0), axis=1
+        ),
         lax.all_gather(decode_queries[0], "ctx", axis=1, tiled=True),
     )
     head_total = window_all.shape[1] // HEAD_DIMENSION

time: 343 us -> 340 us (level)
  waiting for transfers between devices: 107 us -> 98.9 us
  starting transfers between devices: 24.4 us -> 30.7 us
    all_gather x1 -> x0, waiting for transfers between devices: 18 us -> none  [on_device(): lax.all_gather(window_local, 'ctx', axis=1, tiled=True)]
    all_to_all x0 -> x1, waiting for transfers between devices: none -> 9.17 us  [on_device(): lax.all_to_all(jnp.stack([window_local] * lax.axis_size('ctx')), 'ctx', 0...]
    all_to_all x0 -> x1, starting transfers between devices: none -> 6.57 us  [on_device(): lax.all_to_all(jnp.stack([window_local] * lax.axis_size('ctx')), 'ctx', 0...]
where the time goes in v1:
time: 340 us; the launch traced here: 336 us
  waiting for transfers between devices  98.9 us (29%)
  local copies, waits for them, and re-layouts  65.3 us (19%)
  other arithmetic  54 us (16%)
  blocking collectives  47.2 us (14%)
  starting transfers between devices  30.7 us (9%)
  matrix products  22.9 us (7%)
  between operations  15.4 us (5%)
    all_gather x1, waiting for transfers between devices, on_device(): lax.all_gather(decode_queries[0], 'ctx', axis=1, tiled=True)  48.5 us
    all_gather x2, blocking collectives, combined_all(): gathered = jax.tree.map(lambda a: lax.all_gather(a, axis), part)  47.2 us
    all_to_all x1, waiting for transfers between devices, on_device(): lax.all_to_all(cache_acc[None], 'ctx', split_axis=2, concat_axis=0, tiled...  30.1 us
    add x31, other arithmetic, merge_stats(): earlier[1] * jnp.exp(earlier[0] - highest)  25.3 us
    unnamed x87, local copies, waits for them, and re-layouts  12 us
    another operation x2, local copies, waits for them, and re-layouts, on_device(): cache_acc[None]  11.9 us
    dot_general x8, matrix products, on_device(): jnp.einsum('wgd,td->gwt', head_queries, key_head_rows, preferred_element_...  11.5 us
    all_to_all x1, waiting for transfers between devices, on_device(): lax.all_to_all(jnp.stack([window_local] * lax.axis_size('ctx')), 'ctx', 0...  9.17 us
  transfers between devices with their start and end apart: 8, of which 5 were waited for; matrix products, arithmetic and copies ran while one was open for 21% of the time, Pallas kernels for 0%

profile of v1, /device:TPU:25, one launch (start us, length us, event | category | flops | bytes accessed | tf_op | source)
XLA Modules:
  0.0 336.4 jit_solution(8306793333735244190)
XLA Ops:
  13.5 48.5 %all-gather.6.cloned.1.call-done = bf16[1,4,32,8192]{3,1,0,2:T(4,128)(2,1)} async-done(((bf16[1,4,1,8192]{3,1,0,2:T(4,128)(2,1)}), bf16[1,4,32,8192]{3,1,0,2:T(4,128)(2,1)}) %all-gather.6.cloned.1.call-update) | async-done | bytes 2097168 | tf_op jit(solution)/shard_map/all_gather | solution.py:114
  69.3 12.0 %while.34 = (s32[]{:T(128)}, f32[128,8,8]{0,2,1:T(8,128)S(1)}, f32[128,8,8]{0,2,1:T(8,128)S(1)}, f32[128,8,8,128]{3,0,2,1:T(8,128)}, s32[]{:T(128)}, /*index=5*/...) while((s32[]{:T(128)}, f32[128,8,8]{0,2,1:T(8,128)S(1)}, ...), condition=%wide.region_23.24_spmd, body=%wide.region_20.23_spmd.sunk | while | flops 1893744640 | bytes 57671904 | solution.py:205
  73.2 5.4 %bitcast_add_fusion.2 = f32[128,8,8,128]{3,0,2,1:T(8,128)S(1)} fusion(f32[128,8,8,128]{3,0,2,1:T(8,128)S(1)} %copy-done.1, f32[128,8,8]{0,2,1:T(8,128)S(1)} %get-tuple-element.508, f32[8,128,128,8]{2,1,3,0:T(8,128)S(1)} %get-tuple-element.506, f32[128,8,8]{0,2,1:T(8,128)S(1)} %max.37, pred[8]{0:T(512)(128)(4,1)S(1)} %broadcast_compare_fusion.3, ...), kind=kOutput, calls=%fused_computation.7.clone.1 | convolution fusion | flops 1616904192 | bytes 12910600 | tf_op jit(solution)/shard_map/while/body/rhgt,htd->rhgd/dot_general | solution.py:192
  82.3 5.7 %all-to-all-start.2 = ((f32[32,1,256]{2,1,0:T(1,128)}), f32[32,1,256]{2,1,0:T(1,128)S(1)}, u32[]{:S(2)}, u32[]{:S(2)}) async-start(f32[32,1,256]{2,1,0:T(1,128)} %reshape.480), calls=%async_computation.2 | async-start | bytes 65536 | tf_op jit(solution)/shard_map/all_to_all | solution.py:240
  89.0 4.6 %all-to-all-done.2 = f32[32,1,256]{2,1,0:T(1,128)S(1)} async-done(((f32[32,1,256]{2,1,0:T(1,128)}), f32[32,1,256]{2,1,0:T(1,128)S(1)}, u32[]{:S(2)}, u32[]{:S(2)}) %all-to-all-start.2) | async-done | bytes 32800 | tf_op jit(solution)/shard_map/all_to_all | solution.py:240
  93.6 5.6 %all-to-all-start.3 = ((f32[32,1,256]{2,1,0:T(1,128)}), f32[32,1,256]{2,1,0:T(1,128)S(1)}, u32[]{:S(2)}, u32[]{:S(2)}) async-start(f32[32,1,256]{2,1,0:T(1,128)} %reshape.482), calls=%async_computation.3 | async-start | bytes 65536 | tf_op jit(solution)/shard_map/all_to_all | solution.py:241
  99.2 6.6 %copy.206 = f32[128,8,8,128]{3,2,1,0:T(8,128)} copy(f32[128,8,8,128]{3,0,2,1:T(8,128)} %get-tuple-element.265) | data formatting | bytes 8388608 | tf_op jit(solution)/shard_map/while | solution.py:205
  105.9 5.0 %broadcast_in_dim_reshape.10 = f32[1,4,32,8192]{3,2,1,0:T(8,128)} reshape(f32[128,8,8,128]{3,2,1,0:T(8,128)} %copy.206) | data formatting | bytes 8388608 | tf_op jit(solution)/shard_map/broadcast_in_dim;reshape | solution.py:239
  110.8 6.9 %copy.207 = f32[1,4,32,8192]{3,1,0,2:T(4,128)} copy(f32[1,4,32,8192]{3,2,1,0:T(8,128)} %broadcast_in_dim_reshape.10) | data formatting | bytes 8388608 | tf_op jit(solution)/shard_map/broadcast_in_dim;reshape | solution.py:239
  117.8 7.7 %all-to-all-start.1 = ((f32[1,4,32,8192]{3,1,0,2:T(4,128)}), f32[1,4,32,8192]{3,1,0,2:T(4,128)}, u32[]{:S(2)}, u32[]{:S(2)}) async-start(f32[1,4,32,8192]{3,1,0,2:T(4,128)} %copy.207), calls=%async_computation.1 | async-start | bytes 8388608 | tf_op jit(solution)/shard_map/all_to_all | solution.py:239
  132.4 5.5 %mul.308 = f32[32,1,4,1,8192]{4,2,0,3,1:T(4,128)} reshape(f32[32,4,64,128]{3,2,1,0:T(8,128)} %mul.307) | data formatting | bytes 8388608 | tf_op jit(solution)/shard_map/mul | solution.py:249
  138.0 6.4 %copy.181 = bf16[256,8192]{1,0:T(8,128)(2,1)} copy(bf16[256,8192]{0,1:T(8,128)(2,1)} %bitcast.319) | data formatting | bytes 8388608 | tf_op jit(solution)/shard_map/dot_general | solution.py:95
  144.3 3.6 %fusion.40 = f32[64,2,128]{2,0,1:T(8,128)S(1)} fusion(bf16[2,128,8192]{2,1,0:T(8,128)(2,1)} %bitcast.316, bf16[1,64,8192]{2,1,0:T(8,128)(2,1)S(1)} %copy-done), kind=kOutput, calls=%fused_computation.69 | convolution fusion | flops 268435456 | bytes 5308416 | tf_op jit(solution)/shard_map/dot_general | solution.py:95
  148.1 30.1 %all-to-all-done.1 = f32[1,4,32,8192]{3,1,0,2:T(4,128)} async-done(((f32[1,4,32,8192]{3,1,0,2:T(4,128)}), f32[1,4,32,8192]{3,1,0,2:T(4,128)}, u32[]{:S(2)}, u32[]{:S(2)}) %all-to-all-start.1) | async-done | bytes 4194336 | tf_op jit(solution)/shard_map/all_to_all | solution.py:239
  179.3 6.6 %all-to-all-start = ((bf16[32,64,256]{2,1,0:T(8,128)(2,1)}), bf16[32,64,256]{2,1,0:T(8,128)(2,1)S(1)}, u32[]{:S(2)}, u32[]{:S(2)}) async-start(bf16[32,64,256]{2,1,0:T(8,128)(2,1)} %stack.56), calls=%async_computation | async-start | bytes 2097152 | tf_op jit(solution)/shard_map/all_to_all | solution.py:112
  185.9 5.2 %fusion.21 = f32[4,8192]{1,0:T(4,128)S(1)} fusion(f32[32,1,4,1,8192]{4,2,0,3,1:T(4,128)} %mul.308, f32[1,4,32,8192]{3,1,0,2:T(4,128)} %all-to-all-done.1), kind=kLoop, calls=%fused_computation.32 | loop fusion | flops 2064384 | bytes 8519680 | tf_op jit(solution)/shard_map/reduce_sum | solution.py:249
  192.2 9.2 %all-to-all-done = bf16[32,64,256]{2,1,0:T(8,128)(2,1)S(1)} async-done(((bf16[32,64,256]{2,1,0:T(8,128)(2,1)}), bf16[32,64,256]{2,1,0:T(8,128)(2,1)S(1)}, u32[]{:S(2)}, u32[]{:S(2)}) %all-to-all-start) | async-done | bytes 1048608 | tf_op jit(solution)/shard_map/all_to_all | solution.py:112
  214.6 3.6 %fusion.49 = (f32[8,64]{0,1:T(8,128)S(1)}, f32[8,64]{0,1:T(8,128)}, f32[8,64]{0,1:T(8,128)}, f32[8,64]{0,1:T(8,128)}, f32[8,64]{0,1:T(8,128)}, /*index=5*/f32[8,...) fusion(f32[8,64,512]{2,0,1:T(8,128)S(1)} %get-tuple-element.407, f32[8,64]{0,1:T(8,128)S(1)} %get-tuple-element.406, ...), kind=kLoop, calls=%fused_computation.86 | loop fusion | flops 6287360 | bytes 8454144 | tf_op jit(solution)/shard_map/reduce_sum | solution.py:147
  228.6 23.6 %all_gather.14 = f32[32,64,64]{2,1,0:T(8,128)S(1)} all-gather(f32[1,64,64]{2,1,0:T(8,128)} %bitcast.370), channel_id=1, replica_groups=mesh['ctx'=32,'grp'=8] {'ctx'}, dimensions={0}, use_global_device_ids=true | all-gather | bytes 540672 | tf_op jit(solution)/shard_map/all_gather | solution.py:14
  253.8 23.6 %all_gather.13 = f32[32,64,64]{2,1,0:T(8,128)S(1)} all-gather(f32[1,64,64]{2,1,0:T(8,128)S(1)} %bitcast.355), channel_id=1, replica_groups=mesh['ctx'=32,'grp'=8] {'ctx'}, dimensions={0}, use_global_device_ids=true | all-gather | bytes 540672 | tf_op jit(solution)/shard_map/all_gather | solution.py:14
  278.4 25.9 %while.33 = (s32[]{:T(128)}, f32[64,64]{1,0:T(8,128)S(1)}, f32[64,64]{1,0:T(8,128)S(1)}, f32[32,64,64]{2,1,0:T(8,128)}, f32[32,64,64]{2,1,0:T(8,128)}, /*index=5*/s32[]{:T(128)}, s32[]{:T(128)}, s32[]{:T(128)}) while((s32[]{:T(128)}, f32[64,64]{1,0:T(8,128)S(1)}, f32[64,64]{1,0:T(8,128)S(1)}, f32[32,64,64]{2,1,0:T(8,128)}, ...), condition=%wide.region_17.18_spmd, body=%wide.region_16.17_spmd.sunk | while | flops 24581 | bytes 98435 | solution.py:19
  314.8 3.8 %multiply_reduce_fusion = f32[8,512]{1,0:T(8,128)S(1)} fusion(f32[8,8,64,512]{3,1,2,0:T(8,128)} %bitcast_dynamic-update-slice_fusion, f32[8,8,64]{1,2,0:T(8,128)S(1)} %copy.200), kind=kLoop, calls=%fused_computation.30 | loop fusion | flops 4190208 | bytes 8421376 | tf_op jit(solution)/shard_map/reduce_sum | solution.py:155
  318.7 3.1 collective-permute-start
  323.7 5.1 %collective-permute-done.1 = f32[8,3]{1,0:T(8,128)S(1)} collective-permute-done((f32[8,3]{1,0:T(8,128)S(1)}, f32[8,3]{1,0:T(8,128)S(1)}, u32[]{:S(2)}, u32[]{:S(2)}) %collective-permute-start.1) | collective-permute-done | bytes 128 | tf_op jit(solution)/shard_map/ppermute | solution.py:34
  (224 shorter events, 93.6 us)
Async XLA Ops:
  7.2 137.2 %copy-start = (bf16[1,64,8192]{2,1,0:T(8,128)(2,1)S(1)}, bf16[1,64,8192]{2,1,0:T(8,128)(2,1)}, u32[]{:S(2)}) copy-start(bf16[1,64,8192]{2,1,0:T(8,128)(2,1)} %param.14) | copy-start | bytes 3145732
  7.2 54.9 %all-gather.6.cloned.1.call-start = ((), (), s32[]{:S(2)}) async-start(), calls=%async_computation.5 | async-start | bytes 2162688 | tf_op jit(solution)/shard_map/all_gather | solution.py:114
  7.9 130.0 %all-gather.4.cloned.1.call-start = ((), (), s32[]{:S(2)}) async-start(), calls=%async_computation.4 | async-start | bytes 4718592 | tf_op jit(solution)/shard_map/all_gather | solution.py:97
  82.3 11.3 %all-to-all-start.2 = ((f32[32,1,256]{2,1,0:T(1,128)}), f32[32,1,256]{2,1,0:T(1,128)S(1)}, u32[]{:S(2)}, u32[]{:S(2)}) async-start(f32[32,1,256]{2,1,0:T(1,128)} %reshape.480), calls=%async_computation.2 | async-start | bytes 65536 | tf_op jit(solution)/shard_map/all_to_all | solution.py:240
  93.6 24.2 %all-to-all-start.3 = ((f32[32,1,256]{2,1,0:T(1,128)}), f32[32,1,256]{2,1,0:T(1,128)S(1)}, u32[]{:S(2)}, u32[]{:S(2)}) async-start(f32[32,1,256]{2,1,0:T(1,128)} %reshape.482), calls=%async_computation.3 | async-start | bytes 65536 | tf_op jit(solution)/shard_map/all_to_all | solution.py:241
  117.7 8.3 %copy-start.24 = (bf16[1,1,64,1024]{3,2,1,0:T(8,128)(2,1)S(1)}, bf16[1,1,64,1024]{3,2,1,0:T(8,128)(2,1)}, u32[]{:S(2)}) copy-start(bf16[1,1,64,1024]{3,2,1,0:T(8,128)(2,1)} %param.21) | copy-start | bytes 393220
  117.7 8.5 %copy-start.26 = (bf16[1,4,1,8192]{3,1,2,0:T(4,128)(2,1)S(1)}, bf16[1,4,1,8192]{3,1,2,0:T(4,128)(2,1)}, u32[]{:S(2)}) copy-start(bf16[1,4,1,8192]{3,1,2,0:T(4,128)(2,1)} %param.20) | copy-start | bytes 196612
  117.7 9.1 %copy-start.25 = (bf16[1,1,64,1024]{3,2,1,0:T(8,128)(2,1)S(1)}, bf16[1,1,64,1024]{3,2,1,0:T(8,128)(2,1)}, u32[]{:S(2)}) copy-start(bf16[1,1,64,1024]{3,2,1,0:T(8,128)(2,1)} %param.22) | copy-start | bytes 393220
  117.8 60.4 %all-to-all-start.1 = ((f32[1,4,32,8192]{3,1,0,2:T(4,128)}), f32[1,4,32,8192]{3,1,0,2:T(4,128)}, u32[]{:S(2)}, u32[]{:S(2)}) async-start(f32[1,4,32,8192]{3,1,0,2:T(4,128)} %copy.207), calls=%async_computation.1 | async-start | bytes 8388608 | tf_op jit(solution)/shard_map/all_to_all | solution.py:239
  179.3 22.1 %all-to-all-start = ((bf16[32,64,256]{2,1,0:T(8,128)(2,1)}), bf16[32,64,256]{2,1,0:T(8,128)(2,1)S(1)}, u32[]{:S(2)}, u32[]{:S(2)}) async-start(bf16[32,64,256]{2,1,0:T(8,128)(2,1)} %stack.56), calls=%async_computation | async-start | bytes 2097152 | tf_op jit(solution)/shard_map/all_to_all | solution.py:112
  207.0 7.6 %copy-start.3 = (f32[8,64,512]{2,0,1:T(8,128)}, f32[8,64,512]{2,0,1:T(8,128)S(1)}, u32[]{:S(2)}) copy-start(f32[8,64,512]{2,0,1:T(8,128)S(1)} %get-tuple-element.399) | copy-start | bytes 3145732
  208.6 9.6 %copy-start.5 = (f32[8,64,512]{2,0,1:T(8,128)}, f32[8,64,512]{2,0,1:T(8,128)S(1)}, u32[]{:S(2)}) copy-start(f32[8,64,512]{2,0,1:T(8,128)S(1)} %get-tuple-element.401) | copy-start | bytes 3145732
  208.6 44.8 %copy-start.16 = (f32[8,64]{0,1:T(8,128)}, f32[8,64]{0,1:T(8,128)S(1)}, u32[]{:S(2)}) copy-start(f32[8,64]{0,1:T(8,128)S(1)} %get-tuple-element.400) | copy-start | bytes 6148
  210.2 8.1 %copy-start.7 = (f32[8,64,512]{2,0,1:T(8,128)}, f32[8,64,512]{2,0,1:T(8,128)S(1)}, u32[]{:S(2)}) copy-start(f32[8,64,512]{2,0,1:T(8,128)S(1)} %get-tuple-element.403) | copy-start | bytes 3145732
  210.2 43.4 %copy-start.18 = (f32[8,64]{0,1:T(8,128)}, f32[8,64]{0,1:T(8,128)S(1)}, u32[]{:S(2)}) copy-start(f32[8,64]{0,1:T(8,128)S(1)} %get-tuple-element.402) | copy-start | bytes 6148
  211.7 6.5 %copy-start.9 = (f32[8,64,512]{2,0,1:T(8,128)}, f32[8,64,512]{2,0,1:T(8,128)S(1)}, u32[]{:S(2)}) copy-start(f32[8,64,512]{2,0,1:T(8,128)S(1)} %get-tuple-element.405) | copy-start | bytes 3145732
  211.7 41.9 %copy-start.20 = (f32[8,64]{0,1:T(8,128)}, f32[8,64]{0,1:T(8,128)S(1)}, u32[]{:S(2)}) copy-start(f32[8,64]{0,1:T(8,128)S(1)} %get-tuple-element.404) | copy-start | bytes 6148
  213.3 40.4 %copy-start.22 = (f32[8,64]{0,1:T(8,128)}, f32[8,64]{0,1:T(8,128)S(1)}, u32[]{:S(2)}) copy-start(f32[8,64]{0,1:T(8,128)S(1)} %get-tuple-element.406) | copy-start | bytes 6148
  305.8 5.1 %copy-start.8 = (f32[8,64,512]{2,0,1:T(8,128)S(1)}, f32[8,64,512]{2,0,1:T(8,128)}, u32[]{:S(2)}) copy-start(f32[8,64,512]{2,0,1:T(8,128)} %copy-done.7) | copy-start | bytes 3145732
  305.8 5.1 %copy-start.19 = (f32[8,64]{0,1:T(8,128)S(1)}, f32[8,64]{0,1:T(8,128)}, u32[]{:S(2)}) copy-start(f32[8,64]{0,1:T(8,128)} %copy-done.18) | copy-start | bytes 6148
  308.4 5.1 %copy-start.12 = (f32[8,64,512]{2,0,1:T(8,128)S(1)}, f32[8,64,512]{2,0,1:T(8,128)}, u32[]{:S(2)}) copy-start(f32[8,64,512]{2,0,1:T(8,128)} %copy-done.11) | copy-start | bytes 3145732
  308.4 5.1 %copy-start.23 = (f32[8,64]{0,1:T(8,128)S(1)}, f32[8,64]{0,1:T(8,128)}, u32[]{:S(2)}) copy-start(f32[8,64]{0,1:T(8,128)} %copy-done.22) | copy-start | bytes 6148
  318.7 5.1 %collective-permute-start = (f32[8,3]{1,0:T(8,128)S(1)}, f32[8,3]{1,0:T(8,128)S(1)}, u32[]{:S(2)}, u32[]{:S(2)}) collective-permute-start(f32[8,3]{1,0:T(8,128)S(1)} %get-tuple-element.388), channel_id=1, source_target_pairs={{0,8},{8,16},{16,24},{24,32},{32,40},{40,48},{48,56},{56,64},{64,7... | collective-permute-start | bytes 296 | tf_op jit(solution)/shard_map/ppermute | solution.py:32
  321.8 7.0 %collective-permute-start.1 = (f32[8,3]{1,0:T(8,128)S(1)}, f32[8,3]{1,0:T(8,128)S(1)}, u32[]{:S(2)}, u32[]{:S(2)}) collective-permute-start(f32[8,3]{1,0:T(8,128)S(1)} %get-tuple-element.389), channel_id=1, source_target_pairs={{8,0},{16,8},{24,16},{32,24},{40,32},{48,40},{56,48},{64,56},{72,6... | collective-permute-start | bytes 296 | tf_op jit(solution)/shard_map/ppermute | solution.py:34
  (13 other events, 40.9 us)
Sparse Core Ops, SparseCore 0:
  10.6 51.4 all-gather.5
  63.9 54.1 all-gather.3
